TPU v7x, 128 devices: a whole 4x4x4 slice. The times are simulated.
128 devices in a mesh: dp: 4 (over y), tp: 32 (over z, x, core).
Axes of the slice: x: 4, y: 4, z: 4, core: 2. Of those that a mesh axis runs over, the one named last changes fastest.
Arguments:
- activations: bfloat16 [16384, 8192], P('dp', 'tp'), may hold values from -6 to 6
- out_grads: bfloat16 [16384, 8192], P('dp'), may hold values from -0.09375 to 0.09375
- residual: bfloat16 [32768, 8192], P(('dp', 'tp')), may hold values from -6 to 6
- query_factor: float32 [8192, 64], replicated, may hold values from -0.0625 to 0.0625
Outputs:
- new_error: bfloat16 [32768, 8192], P(('dp', 'tp'))
- right_new: float32 [8192, 64], replicated
All inputs are finite; a program needn't handle non-finite values.
Results may differ from a plain program's by a relative error of at most 0.001.
Values sent between devices are 32-bit elements; how exact they have to be, the bound alone decides.
A program may use at most 192 MiB of HBM per device.

v0:
```python
import jax
import jax.numpy as jnp
from jax import lax
from jax.sharding import PartitionSpec as P


def replica_mean(partial_left):
    return lax.psum(partial_left, "dp") / lax.axis_size("dp")


def on_device(activations, out_grads, residual, query_factor):
    highest = lax.Precision.HIGHEST
    gradient = jnp.dot(activations.T, out_grads, preferred_element_type=jnp.float32)
    merged = gradient + residual.astype(jnp.float32)
    averaged = replica_mean(jnp.dot(merged, query_factor, precision=highest))
    gram_matrix = lax.psum(jnp.dot(averaged.T, averaged, precision=highest), "tp")
    cholesky_lower = jnp.linalg.cholesky(gram_matrix)
    orthonormal = lax.linalg.triangular_solve(
        cholesky_lower, averaged, left_side=False, lower=True, transpose_a=True
    )
    right_terms = jnp.dot(merged.T, orthonormal, precision=highest)
    right_new = lax.psum(right_terms, ("dp", "tp")) / lax.axis_size("dp")
    new_error = (merged - jnp.dot(orthonormal, right_new.T, precision=highest)).astype(jnp.bfloat16)
    return (new_error, right_new)


def solution(mesh):
    return jax.shard_map(
        on_device,
        mesh=mesh,
        in_specs=(P("dp", "tp"), P("dp", None), P(("dp", "tp"), None), P()),
        out_specs=(P(("dp", "tp"), None), P()),
        check_vma=False,
    )
```

profile of v0, /device:TPU:1, one launch (start us, length us, event | category | flops | bytes accessed | tf_op | source)
XLA Modules:
  0.0 412.2 jit_solution(3508932866810993405)
XLA Ops:
  7.2 0.0 copy-start
  7.2 0.0 all-reduce.3.cloned.1.call-start
  7.2 1.5 copy-done
  8.8 31.4 %convolution_add_fusion = f32[256,8192]{1,0:T(8,128)} fusion(bf16[4096,256]{1,0:T(8,128)(2,1)S(1)} %copy-done, bf16[4096,8192]{1,0:T(8,128)(2,1)} %param.5, bf16[256,8192]{1,0:T(8,128)(2,1)} %param.6), kind=kOutput, calls=%fused_computation.1 | convolution fusion | flops 17184063488 | bytes 81788928 | tf_op jit(solution)/shard_map/dot_general | solution.py:13
  40.2 0.0 copy-done.2
  40.2 10.7 %fusion.12 = f32[256,64]{0,1:T(8,128)} fusion(f32[256,8192]{1,0:T(8,128)} %convolution_add_fusion, f32[8192,64]{0,1:T(8,128)S(1)} %copy-done.2), kind=kOutput, calls=%fused_computation.21 | convolution fusion | flops 1610612736 | bytes 10551296 | tf_op jit(solution)/shard_map/dot_general | solution.py:15
  50.8 0.0 all-reduce.3.cloned.1.call-update
  50.9 0.0 all-reduce.5.cloned.1.call-start
  50.9 42.1 %all-reduce.3.cloned.1.call-done = f32[256,64]{0,1:T(8,128)} async-done(((f32[256,64]{0,1:T(8,128)}), f32[256,64]{0,1:T(8,128)}) %all-reduce.3.cloned.1.call-update) | async-done | bytes 65552 | tf_op jit(solution)/shard_map/psum | solution.py:8
  93.0 1.1 fusion.3
  94.2 123.4 %psum.22 = f32[64,64]{0,1:T(8,128)S(1)} all-reduce(f32[64,64]{0,1:T(8,128)S(1)} %fusion.3), channel_id=1, replica_groups=mesh['dp'=4,'tp'=32] {'tp'}, use_global_device_ids=true, to_apply=%region_1.0 | all-reduce | flops 4096 | bytes 32768 | tf_op jit(solution)/shard_map/psum | solution.py:16
  217.6 0.1 copy.7
  217.7 5.8 %cholesky.16 = f32[64,64]{1,0:T(8,128)S(1)} custom-call(f32[64,64]{1,0:T(8,128)S(1)} %fusion.7), custom_call_target="Cholesky" | custom-call | tf_op jit(solution)/shard_map/jit(cholesky)/cholesky | solution.py:17
  223.6 0.6 compare_reduce_fusion
  224.2 0.7 fusion.5
  224.9 4.9 %custom-call.6 = f32[1,64,64]{1,2,0:T(8,128)S(1)} custom-call(f32[1,64,64]{2,1,0:T(8,128)S(1)} %fusion.5), custom_call_target="InvertDiagBlocksLowerTriangular" | custom-call | tf_op jit(solution)/shard_map/triangular_solve | solution.py:18
  229.8 1.1 fusion.1
  230.9 10.1 %fusion.13 = f32[8192,64]{0,1:T(8,128)} fusion(f32[256,8192]{1,0:T(8,128)} %convolution_add_fusion, f32[256,64]{0,1:T(8,128)S(1)} %fusion.1), kind=kOutput, calls=%fused_computation.22 | convolution fusion | flops 1610612736 | bytes 10551296 | tf_op jit(solution)/shard_map/dot_general | solution.py:21
  241.0 0.0 all-reduce.5.cloned.1.call-update
  241.1 151.1 %all-reduce.5.cloned.1.call-done = f32[8192,64]{0,1:T(8,128)} async-done(((f32[8192,64]{0,1:T(8,128)}), f32[8192,64]{0,1:T(8,128)}) %all-reduce.5.cloned.1.call-update) | async-done | bytes 2097168 | tf_op jit(solution)/shard_map/psum | solution.py:22
  392.2 1.8 broadcast_multiply_fusion
  393.9 0.0 copy-start.1
  394.0 11.4 %fusion = bf16[256,8192]{1,0:T(8,128)(2,1)} fusion(f32[256,8192]{1,0:T(8,128)} %convolution_add_fusion, f32[256,64]{0,1:T(8,128)S(1)} %fusion.1, f32[8192,64]{0,1:T(8,128)S(1)} %broadcast_multiply_fusion), kind=kOutput, calls=%fused_computation.2 | convolution fusion | flops 1614807040 | bytes 14745600 | tf_op jit(solution)/shard_map/dot_general | solution.py:23
  405.4 0.0 copy-done.1
  (3 shorter events, 0.0 us)
Async XLA Ops:
  7.2 1.6 copy-start
  7.2 85.9 %all-reduce.3.cloned.1.call-start = ((), (), s32[]{:S(2)}) async-start(), calls=%async_computation | async-start | bytes 131072 | tf_op jit(solution)/shard_map/psum | solution.py:8
  8.8 31.4 %copy-start.2 = (f32[8192,64]{0,1:T(8,128)S(1)}, f32[8192,64]{0,1:T(8,128)}, u32[]{:S(2)}) copy-start(f32[8192,64]{0,1:T(8,128)} %param.7) | copy-start | bytes 6291460
  50.9 341.3 %all-reduce.5.cloned.1.call-start = ((), (), s32[]{:S(2)}) async-start(), calls=%async_computation.1 | async-start | bytes 4194304 | tf_op jit(solution)/shard_map/psum | solution.py:22
  393.9 11.5 %copy-start.1 = (f32[8192,64]{0,1:T(8,128)}, f32[8192,64]{0,1:T(8,128)S(1)}, u32[]{:S(2)}) copy-start(f32[8192,64]{0,1:T(8,128)S(1)} %broadcast_multiply_fusion) | copy-start | bytes 6291460
Sparse Core Ops, SparseCore 0:
  51.0 42.0 all-reduce.2
  241.2 150.9 all-reduce.4
where the time goes:
time: 413 us; the launch traced here: 412 us
  waiting for transfers between devices  193 us (47%)
  blocking collectives  123 us (30%)
  matrix products  65.9 us (16%)
  between operations  14.1 us (3%)
  other arithmetic  13.8 us (3%)
    psum x1, waiting for transfers between devices, on_device(): right_new = lax.psum(right_terms, ('dp', 'tp')) / lax.axis_size('dp')  151 us
    psum x1, blocking collectives, on_device(): lax.psum(jnp.dot(averaged.T, averaged, precision=highest), 'tp')  123 us
    psum x1, waiting for transfers between devices, replica_mean(): return lax.psum(partial_left, 'dp') / lax.axis_size('dp')  42.1 us
    dot_general x1, matrix products, on_device(): jnp.dot(activations.T, out_grads, preferred_element_type=jnp.float32)  31.4 us
    dot_general x1, matrix products, on_device(): jnp.dot(orthonormal, right_new.T, precision=highest)  11.4 us
    dot_general x1, matrix products, on_device(): averaged = replica_mean(jnp.dot(merged, query_factor, precision=highest))  10.7 us
    dot_general x1, matrix products, on_device(): right_terms = jnp.dot(merged.T, orthonormal, precision=highest)  10.1 us
  transfers between devices with their start and end apart: 2, of which 2 were waited for; matrix products, arithmetic and copies ran while one was open for 0% of the time, Pallas kernels for 0%

commit v1 on v0

v1 whole, which is shorter than its diff:
```python
import functools

import jax
import jax.numpy as jnp
from jax import lax
from jax.experimental import pallas as pl
from jax.experimental.pallas import tpu as pltpu
from jax.sharding import PartitionSpec as P

MESH = pl.DeviceIdType.MESH
F32, BF16 = jnp.float32, jnp.bfloat16
HIGHEST = lax.Precision.HIGHEST
TILE = 1024
GROUPS = 4
AXES = ("x", "z", "y", "x")
PHASES = ("core", "line", "plane", "ag_plane", "ag_line", "ag_core")
N_SEMS = 5 + GROUPS * len(PHASES)


def halves(v):
    high = v.astype(BF16)
    return high, (v - high.astype(F32)).astype(BF16)


def thirds(v):
    high = v.astype(BF16)
    rest = v - high.astype(F32)
    mid = rest.astype(BF16)
    return high, mid, (rest - mid.astype(F32)).astype(BF16)


def dot(a, b, ca, cb, precision=None):
    return lax.dot_general(a, b, (((ca,), (cb,)), ((), ())), precision=precision, preferred_element_type=F32)


def kernel(sizes, act_hbm, grad_hbm, res_hbm, query_hbm, error_hbm, right_hbm,
           act, gbuf, res, query, query3, gslice, merged, gq, left, avg, avg2, gram_in, gram_out, gram_slots, chol,
           wl3, tt, core_rx, line_rx, line_sum, plane_rx, tf, right, send, recv, load, gload, store):
    ny, nz, nx = sizes["y"], sizes["z"], sizes["x"]
    dp, tp = lax.axis_index("dp"), lax.axis_index("tp")
    me = {"y": dp, "z": tp // (2 * nx), "x": (tp // 2) % nx}
    core = tp % 2
    rank, width = query_hbm.shape
    tokens, rows = act_hbm.shape
    n_tiles = width // TILE
    gcols = width // GROUPS
    half = rank // 2

    def device(**to):
        at = {**me, "c": core, **to}
        return (at["y"], (at["z"] * nx + at["x"]) * 2 + at["c"])

    def shift(axis, k):
        return lax.rem(me[axis] + k, sizes[axis])

    partner = device(c=1 - core)
    chip = me["z"] * nx + me["x"]
    n_plane = nz * nx

    def to_plane(b1, b2, act_on):
        n2 = sizes[b2]

        @pl.loop(1, sizes[b1] * n2)
        def _(k):
            p1, p2 = shift(b1, k // n2), shift(b2, k % n2)
            act_on(device(**{b1: p1, b2: p2}), p1 * n2 + p2)

    def to_line(axis, act_on):
        @pl.loop(1, sizes[axis])
        def _(k):
            p = shift(axis, k)
            act_on(device(**{axis: p}), p)

    sent = []

    def remote(src, dst, sem, dev):
        pltpu.make_async_remote_copy(
            src_ref=src, dst_ref=dst, send_sem=send.at[sem], recv_sem=recv.at[sem], device_id=dev, device_id_type=MESH
        ).start()

    def arrived(view, sem):
        pltpu.make_async_copy(view(), view(), recv.at[sem]).wait()
        sent.append((view, sem))

    def at_group(g):
        return pl.ds(gcols * g, gcols)

    def sem_of(g, phase):
        return 5 + g * len(PHASES) + PHASES.index(phase)

    slot = core * n_plane + chip
    slice_rows = tokens // (2 * n_plane)
    loads = [
        pltpu.make_async_copy(query_hbm, query, load.at[0]),
        pltpu.make_async_copy(grad_hbm.at[pl.ds(pl.multiple_of(slot * slice_rows, slice_rows), slice_rows)], gslice, load.at[1]),
        pltpu.make_async_copy(act_hbm, act, load.at[2]),
        pltpu.make_async_copy(res_hbm, res, load.at[3]),
    ]

    def tile_load(i):
        b = lax.rem(i, 2)
        return pltpu.make_async_copy(grad_hbm.at[:, pl.ds(pl.multiple_of(i * TILE, TILE), TILE)], gbuf.at[b], gload.at[b])

    for c in loads[:3]:
        c.start()
    tile_load(0).start()
    loads[3].start()
    tile_load(1).start()

    barrier = pltpu.get_barrier_semaphore()

    def greet(dev, _):
        pl.semaphore_signal(barrier, inc=1, device_id=dev, device_id_type=MESH)

    greet(partner, 0)
    to_plane("z", "x", greet)

    @pl.loop(1, ny)
    def _(k):
        y = shift("y", k)

        @pl.loop(0, nx)
        def _(j):
            greet(device(y=y, x=shift("x", j)), 0)

        @pl.loop(1, nz)
        def _(j):
            greet(device(y=y, z=shift("z", j)), 0)

    n_greet = 1 + n_plane - 1 + (ny - 1) * (nx + nz - 1)

    loads[0].wait()
    loads[1].wait()

    @pl.loop(0, n_tiles)
    def _(i):
        cols = pl.ds(pl.multiple_of(i * TILE, TILE), TILE)
        for j, part in enumerate(thirds(query[:, cols])):
            query3[j * rank:(j + 1) * rank, cols] = part

    def fold3(v):
        return v[:rank] + (v[rank:2 * rank] + v[2 * rank:])

    gq_cols = pl.ds(pl.multiple_of(slot * slice_rows, slice_rows), slice_rows)
    gq[:, gq_cols] = fold3(dot(query3[...], gslice[...], 1, 1))
    pl.semaphore_wait(barrier, n_greet)
    to_plane("z", "x", lambda dev, _: remote(gq.at[:, gq_cols], gq.at[:, gq_cols], 0, dev))

    def tile(i):
        cols = pl.ds(pl.multiple_of(i * TILE, TILE), TILE)
        tile_load(i).wait()
        product = dot(act[...], gbuf[lax.rem(i, 2)], 0, 0)
        merged[:, cols] = product + res[:, cols].astype(F32)

        @pl.when(i + 2 < n_tiles)
        def _():
            tile_load(i + 2).start()

    def gq_core():
        arrived(lambda: gq.at[:, pl.ds(0, (n_plane - 1) * slice_rows)], 0)
        mine = gq.at[:, pl.ds(pl.multiple_of(core * n_plane * slice_rows, slice_rows), n_plane * slice_rows)]
        remote(mine, mine, 1, partner)

    def left_factor():
        arrived(lambda: gq.at[:, pl.ds(0, n_plane * slice_rows)], 1)
        total = fold3(dot(query3[...], res[...], 1, 1))
        total += fold3(dot(jnp.concatenate(thirds(gq[...]), axis=0), act[...], 1, 0))
        left[dp] = total
        to_line("y", lambda dev, _: remote(left.at[dp], left.at[dp], 2, dev))

    def average():
        arrived(lambda: left.at[pl.ds(0, ny - 1)], 2)
        total = left[0]
        for r in range(1, ny):
            total = total + left[r]
        total = total * (1.0 / ny)
        avg[...] = total
        high, low = halves(total)
        avg2[:rank] = high
        avg2[rank:] = low
        gram = dot(total, total, 1, 1, HIGHEST)
        gram_out[...] = jnp.concatenate([gram[:half], gram[half:]], axis=1)
        remote(gram_out, gram_in, 3, partner)

    def gram_sum():
        arrived(lambda: gram_in, 3)
        gram_slots[chip] = gram_out[...] + gram_in[...]
        to_plane("z", "x", lambda dev, _: remote(gram_slots.at[chip], gram_slots.at[chip], 4, dev))

    def right_terms(g):
        step = 512

        @pl.loop(0, gcols // step)
        def _(i):
            cols = pl.ds(pl.multiple_of(gcols * g + i * step, step), step)
            high, low = halves(merged[:, cols])
            both = dot(avg2[...], high, 1, 0)
            tt[:, cols] = both[:rank] + (both[rank:] + dot(avg2[:rank], low, 1, 0))

        theirs = pl.ds(pl.multiple_of(half * (1 - core), half), half)
        remote(tt.at[theirs, at_group(g)], core_rx.at[:, at_group(g)], sem_of(g, "core"), partner)

    def line_of(g):
        axis = AXES[g]
        b1, b2 = [a for a in ("y", "z", "x") if a != axis]
        n = sizes[axis]
        n_p = sizes[b1] * sizes[b2]
        return axis, b1, b2, n, half // n, me[b1] * sizes[b2] + me[b2], n_p, gcols // n_p

    def part_rows(p, size):
        return pl.ds(pl.multiple_of(p * size, size), size)

    def line_send(g):
        axis, _, _, n, lrows, *_ = line_of(g)
        cols = at_group(g)
        arrived(lambda: core_rx.at[:, cols], sem_of(g, "core"))
        core_rx[:, cols] = core_rx[:, cols] + tt[part_rows(core, half), cols]
        to_line(axis, lambda dev, p: remote(
            core_rx.at[part_rows(p, lrows), cols], line_rx.at[g, part_rows(me[axis], lrows)], sem_of(g, "line"), dev))

    def plane_send(g):
        axis, b1, b2, n, lrows, pos, n_p, pcols = line_of(g)
        arrived(lambda: line_rx.at[g, pl.ds(0, (n - 1) * lrows)], sem_of(g, "line"))
        total = core_rx[part_rows(me[axis], lrows), at_group(g)]
        for k in range(1, n):
            total = total + line_rx[g, part_rows(shift(axis, k), lrows)]
        line_sum[g, :lrows] = total
        to_plane(b1, b2, lambda dev, p: remote(
            line_sum.at[g, pl.ds(0, lrows), part_rows(p, pcols)],
            plane_rx.at[g, pl.ds(0, lrows), part_rows(pos, pcols)], sem_of(g, "plane"), dev))

    def gather_plane(g):
        axis, b1, b2, n, lrows, pos, n_p, pcols = line_of(g)
        rest = pl.ds(0, (n_p - 1) * pcols)
        arrived(lambda: plane_rx.at[g, pl.ds(0, lrows), rest], sem_of(g, "plane"))
        mine = part_rows(pos, pcols)
        plane_rx[g, :lrows, mine] = line_sum[g, :lrows, mine]
        total = plane_rx[g, :lrows, 0:pcols]
        for k in range(1, n_p):
            total = total + plane_rx[g, :lrows, k * pcols:(k + 1) * pcols]
        piece = (pl.ds(pl.multiple_of(half * core + lrows * me[axis], lrows), lrows),
                 pl.ds(pl.multiple_of(gcols * g + pcols * pos, pcols), pcols))
        tf[piece] = total
        to_plane(b1, b2, lambda dev, _: remote(tf.at[piece], tf.at[piece], sem_of(g, "ag_plane"), dev))

    def gather_line(g):
        axis, b1, b2, n, lrows, pos, n_p, pcols = line_of(g)
        arrived(lambda: tf.at[pl.ds(0, lrows), pl.ds(0, (n_p - 1) * pcols)], sem_of(g, "ag_plane"))
        piece = (pl.ds(pl.multiple_of(half * core + lrows * me[axis], lrows), lrows), at_group(g))
        to_line(axis, lambda dev, _: remote(tf.at[piece], tf.at[piece], sem_of(g, "ag_line"), dev))

    def gather_core(g):
        axis, b1, b2, n, lrows, *_ = line_of(g)
        arrived(lambda: tf.at[pl.ds(0, (n - 1) * lrows), at_group(g)], sem_of(g, "ag_line"))
        mine = tf.at[part_rows(core, half), at_group(g)]
        remote(mine, mine, sem_of(g, "ag_core"), partner)

    def cholesky():
        arrived(lambda: gram_slots.at[pl.ds(0, n_plane - 1)], 4)
        packed = gram_slots[0]
        for k in range(1, n_plane):
            packed = packed + gram_slots[k]
        gram = jnp.concatenate([packed[:, :rank], packed[:, rank:]], axis=0)
        at_row = lax.broadcasted_iota(jnp.int32, (rank, 1), 0)
        at_lane = lax.broadcasted_iota(jnp.int32, (1, 2 * rank), 1)
        unit = (lax.broadcasted_iota(jnp.int32, (rank, rank), 0) == lax.broadcasted_iota(jnp.int32, (rank, rank), 1)).astype(F32)
        chol[...] = jnp.concatenate([gram, unit], axis=1)

        @pl.loop(0, rank)
        def _(k):
            matrix = chol[...]
            row = chol[pl.ds(k, 1), :]
            column = jnp.sum(jnp.where(at_lane == k, matrix, 0.0), axis=1, keepdims=True)
            pivot = jnp.sum(jnp.where(at_lane == k, row, 0.0), axis=1, keepdims=True)
            scale = 1.0 / jnp.sqrt(pivot)
            row = row * scale
            chol[...] = jnp.where(at_row == k, row, matrix - jnp.where(at_row > k, column * scale, 0.0) * row)

        inverse = chol[:, rank:]
        orth = dot(inverse, avg[...], 1, 0, HIGHEST)
        both = jnp.concatenate([dot(inverse, orth, 0, 0, HIGHEST), inverse.T, jnp.zeros((rank, rank), F32)], axis=1)
        high, low = halves(both * (1.0 / ny))
        wl3[:rank] = high
        wl3[rank:2 * rank] = high
        wl3[2 * rank:] = low

    def out_copies(g):
        return [pltpu.make_async_copy(res.at[:, at_group(g)], error_hbm.at[:, at_group(g)], store.at[g, 0]),
                pltpu.make_async_copy(right.at[:, at_group(g)], right_hbm.at[:, at_group(g)], store.at[g, 1])]

    def finish(g):
        step = 512
        arrived(lambda: tf.at[pl.ds(0, half), at_group(g)], sem_of(g, "ag_core"))

        @pl.loop(0, gcols // step)
        def _(i):
            cols = pl.ds(pl.multiple_of(gcols * g + i * step, step), step)
            high, low = halves(tf[:, cols])
            both = dot(wl3[...], jnp.concatenate([high, low, high], axis=0), 0, 0)
            res[:, cols] = (merged[:, cols] - both[:rows]).astype(BF16)
            right[:, cols] = both[rows:rows + rank]

        for c in out_copies(g):
            c.start()

    loads[2].wait()
    loads[3].wait()
    early = range(GROUPS - 1)
    last = GROUPS - 1

    def after_5():
        average()
        for g in early:
            right_terms(g)

    def after_6():
        gram_sum()
        for g in early:
            line_send(g)

    def after_7():
        right_terms(last)
        for g in early:
            plane_send(g)

    stages = {2: gq_core, 3: left_factor, 5: after_5, 6: after_6, 7: after_7}

    @pl.loop(0, n_tiles)
    def _(i):
        tile(i)
        for at, stage in stages.items():
            pl.when(i == at)(stage)

    line_send(last)
    for g in early:
        gather_plane(g)
    plane_send(last)
    for g in early:
        gather_line(g)
    cholesky()
    gather_plane(last)
    for g in early:
        gather_core(g)
    gather_line(last)
    for g in early:
        finish(g)
    gather_core(last)
    finish(last)
    for g in range(GROUPS):
        for c in out_copies(g):
            c.wait()
    for view, sem in sent:
        pltpu.make_async_copy(view(), view(), send.at[sem]).wait()


def solution(mesh):
    n_dp, n_tp = mesh.shape["dp"], mesh.shape["tp"]
    nx = 4 if n_tp == 32 else 2
    sizes = {"y": n_dp, "z": n_tp // (2 * nx), "x": nx}

    def on_device(activations, out_grads, residual, query_factor):
        tokens, rows = activations.shape
        width, rank = query_factor.shape
        half = rank // 2
        gcols = width // GROUPS
        n_plane = sizes["z"] * sizes["x"]
        lmax = half // min(sizes.values())
        error, right_t = pl.pallas_call(
            functools.partial(kernel, sizes),
            out_shape=(jax.ShapeDtypeStruct((rows, width), BF16), jax.ShapeDtypeStruct((rank, width), F32)),
            in_specs=[pl.BlockSpec(memory_space=pl.ANY)] * 4,
            out_specs=(pl.BlockSpec(memory_space=pl.ANY),) * 2,
            scratch_shapes=[
                pltpu.VMEM((tokens, rows), BF16),
                pltpu.VMEM((2, tokens, TILE), BF16),
                pltpu.VMEM((rows, width), BF16),
                pltpu.VMEM((rank, width), F32),
                pltpu.VMEM((3 * rank, width), BF16),
                pltpu.VMEM((tokens // (2 * n_plane), width), BF16),
                pltpu.VMEM((rows, width), F32),
                pltpu.VMEM((rank, tokens), F32),
                pltpu.VMEM((n_dp, rank, rows), F32),
                pltpu.VMEM((rank, rows), F32),
                pltpu.VMEM((2 * rank, rows), BF16),
                pltpu.VMEM((half, 2 * rank), F32),
                pltpu.VMEM((half, 2 * rank), F32),
                pltpu.VMEM((n_plane, half, 2 * rank), F32),
                pltpu.VMEM((rank, 2 * rank), F32),
                pltpu.VMEM((3 * rank, rows + 2 * rank), BF16),
                pltpu.VMEM((rank, width), F32),
                pltpu.VMEM((half, width), F32),
                pltpu.VMEM((GROUPS, half, gcols), F32),
                pltpu.VMEM((GROUPS, lmax, gcols), F32),
                pltpu.VMEM((GROUPS, lmax, gcols), F32),
                pltpu.VMEM((rank, width), F32),
                pltpu.VMEM((rank, width), F32),
                pltpu.SemaphoreType.DMA((N_SEMS,)),
                pltpu.SemaphoreType.DMA((N_SEMS,)),
                pltpu.SemaphoreType.DMA((4,)),
                pltpu.SemaphoreType.DMA((2,)),
                pltpu.SemaphoreType.DMA((GROUPS, 2)),
            ],
            compiler_params=pltpu.CompilerParams(
                collective_id=0, has_side_effects=True, vmem_limit_bytes=60 * 2**20
            ),
            name="powersgd",
        )(activations, out_grads, residual, query_factor.T)
        return error, right_t.T

    return jax.shard_map(
        on_device,
        mesh=mesh,
        in_specs=(P("dp", "tp"), P("dp", None), P(("dp", "tp"), None), P()),
        out_specs=(P(("dp", "tp"), None), P()),
        check_vma=False,
    )
```

time: 413 us -> 83.1 us (0.20)
  waiting for transfers between devices: 193 us -> 0 us
  blocking collectives: 123 us -> 0 us
  Pallas kernels: 0 us -> 76.2 us
  matrix products: 65.9 us -> 0 us
  other arithmetic: 13.8 us -> 0 us
  between operations: 14.1 us -> 0.65 us
  local copies, waits for them, and re-layouts: 1.63 us -> 6.11 us
    psum x2 -> x0, waiting for transfers between devices: 193 us -> none  [the longest x1 151 us: on_device(): right_new = lax.psum(right_terms, ('dp', 'tp')) / lax.axis_size('dp')]
    psum x1 -> x0, blocking collectives: 123 us -> none  [on_device(): lax.psum(jnp.dot(averaged.T, averaged, precision=highest), 'tp')]
    pallas_call x0 -> x1, Pallas kernels: none -> 76.2 us  [on_device(): pl.pallas_call(functools.partial(kernel, sizes), out_shape=(jax.ShapeDtyp...]
    dot_general x5 -> x0, matrix products: 64.8 us -> none  [the longest x1 31.4 us: on_device(): jnp.dot(activations.T, out_grads, preferred_element_type=jnp.float32)]
    another operation x5 -> x0, other arithmetic: 12.1 us -> none  [the longest x3 6.52 us: on_device(): cholesky_lower = jnp.linalg.cholesky(gram_matrix)]
    unnamed x6 -> x4, local copies, waits for them, and re-layouts: 1.55 us -> 6.11 us
  transfers between devices with their start and end apart: 2 -> 0, of which waited for: 2 -> 0; matrix products, arithmetic and copies ran while one was open for 0% -> 0% of each run, Pallas kernels for 0% -> 0%
where the time goes in v1:
time: 83.1 us; the launch traced here: 83 us
  Pallas kernels  76.2 us (92%)
  local copies, waits for them, and re-layouts  6.11 us (7%)
    pallas_call x1, Pallas kernels, on_device(): pl.pallas_call(functools.partial(kernel, sizes), out_shape=(jax.ShapeDtyp...  76.2 us
    unnamed x4, local copies, waits for them, and re-layouts  6.11 us

profile of v1, /device:TPU:1, one launch (start us, length us, event | category | flops | bytes accessed | tf_op | source)
XLA Modules:
  0.0 83.0 jit_solution(16334899461910839872)
XLA Ops:
  0.6 76.2 %powersgd.1 = (bf16[256,8192]{1,0:T(8,128)(2,1)}, f32[64,8192]{1,0:T(8,128)}) custom-call(bf16[4096,256]{1,0:T(8,128)(2,1)} %act_hbm.1, bf16[4096,8192]{1,0:T(8,128)(2,1)} %grad_hbm.1, bf16[256,8192]{1,0:T(8,128)(2,1)} %res_hbm.1, f32[64,8192]{1,0:T(8,128)} %bitcast.2), custom_call_target="tpu_custom_call" | custom-call | tf_op jit(solution)/shard_map/powersgd/pallas_call | solution.py:368
  76.9 0.0 copy-start
  76.9 4.8 %copy.8 = bf16[256,8192]{1,0:T(8,128)(2,1)} copy(bf16[256,8192]{1,0:T(8,128)(2,1)} %get-tuple-element.8) | data formatting | bytes 8388608
  81.6 0.0 copy-done
  81.7 1.3 %copy.9 = f32[8192,64]{0,1:T(8,128)} copy(f32[8192,64]{0,1:T(8,128)S(1)} %bitcast.3) | data formatting | bytes 4194304
Async XLA Ops:
  76.9 4.8 %copy-start = (f32[64,8192]{1,0:T(8,128)S(1)}, f32[64,8192]{1,0:T(8,128)}, u32[]{:S(2)}) copy-start(f32[64,8192]{1,0:T(8,128)} %get-tuple-element.5) | copy-start | bytes 6291460

commit v2 on v1

--- a/solution.py
+++ b/solution.py
@@ -12,7 +12,8 @@
 HIGHEST = lax.Precision.HIGHEST
 TILE = 1024
 GROUPS = 4
-AXES = ("x", "z", "y", "x")
+AXES = ("x", "z", "y")
+SLOTS = 3
 PHASES = ("core", "line", "plane", "ag_plane", "ag_line", "ag_core")
 N_SEMS = 5 + GROUPS * len(PHASES)
 
@@ -33,9 +34,10 @@
     return lax.dot_general(a, b, (((ca,), (cb,)), ((), ())), precision=precision, preferred_element_type=F32)
 
 
-def kernel(sizes, act_hbm, grad_hbm, res_hbm, query_hbm, error_hbm, right_hbm,
-           act, gbuf, res, query, query3, gslice, merged, gq, left, avg, avg2, gram_in, gram_out, gram_slots, chol,
-           wl3, tt, core_rx, line_rx, line_sum, plane_rx, tf, right, send, recv, load, gload, store):
+def kernel(sizes, act_hbm, grad_hbm, res_hbm, query_hbm, res, right,
+           act, gbuf, query3, gslice, merged, gq, left, avg, avg2, gram_in, gram_out, gram_slots, chol,
+           wl3, tt, core_rx, line_rx, line_sum, plane_rx, last_rx, tf, send, recv, load, gload):
+    query = right
     ny, nz, nx = sizes["y"], sizes["z"], sizes["x"]
     dp, tp = lax.axis_index("dp"), lax.axis_index("tp")
     me = {"y": dp, "z": tp // (2 * nx), "x": (tp // 2) % nx}
@@ -56,6 +58,8 @@
     partner = device(c=1 - core)
     chip = me["z"] * nx + me["x"]
     n_plane = nz * nx
+    n_chips = ny * n_plane
+    place = dp * n_plane + chip
 
     def to_plane(b1, b2, act_on):
         n2 = sizes[b2]
@@ -71,6 +75,12 @@
             p = shift(axis, k)
             act_on(device(**{axis: p}), p)
 
+    def to_all(act_on):
+        @pl.loop(1, n_chips)
+        def _(k):
+            y, z, x = shift("y", k // n_plane), shift("z", (k // nx) % nz), shift("x", k % nx)
+            act_on(device(y=y, z=z, x=x), (y * nz + z) * nx + x)
+
     sent = []
 
     def remote(src, dst, sem, dev):
@@ -93,19 +103,18 @@
     loads = [
         pltpu.make_async_copy(query_hbm, query, load.at[0]),
         pltpu.make_async_copy(grad_hbm.at[pl.ds(pl.multiple_of(slot * slice_rows, slice_rows), slice_rows)], gslice, load.at[1]),
-        pltpu.make_async_copy(act_hbm, act, load.at[2]),
-        pltpu.make_async_copy(res_hbm, res, load.at[3]),
+        pltpu.make_async_copy(res_hbm, res, load.at[2]),
+        pltpu.make_async_copy(act_hbm, act, load.at[3]),
     ]
 
     def tile_load(i):
-        b = lax.rem(i, 2)
+        b = lax.rem(i, SLOTS)
         return pltpu.make_async_copy(grad_hbm.at[:, pl.ds(pl.multiple_of(i * TILE, TILE), TILE)], gbuf.at[b], gload.at[b])
 
-    for c in loads[:3]:
+    for c in loads:
         c.start()
-    tile_load(0).start()
-    loads[3].start()
-    tile_load(1).start()
+    for b in range(SLOTS):
+        tile_load(b).start()
 
     barrier = pltpu.get_barrier_semaphore()
 
@@ -113,48 +122,47 @@
         pl.semaphore_signal(barrier, inc=1, device_id=dev, device_id_type=MESH)
 
     greet(partner, 0)
-    to_plane("z", "x", greet)
-
-    @pl.loop(1, ny)
-    def _(k):
-        y = shift("y", k)
-
-        @pl.loop(0, nx)
-        def _(j):
-            greet(device(y=y, x=shift("x", j)), 0)
-
-        @pl.loop(1, nz)
-        def _(j):
-            greet(device(y=y, z=shift("z", j)), 0)
-
-    n_greet = 1 + n_plane - 1 + (ny - 1) * (nx + nz - 1)
+    to_all(greet)
+    n_greet = 1 + n_chips - 1
 
     loads[0].wait()
     loads[1].wait()
+
+    def fold3(v):
+        return v[:rank] + (v[rank:2 * rank] + v[2 * rank:])
+
+    gq_cols = pl.ds(pl.multiple_of(slot * slice_rows, slice_rows), slice_rows)
+    gq[:, gq_cols] = jnp.zeros((rank, slice_rows), F32)
 
     @pl.loop(0, n_tiles)
     def _(i):
         cols = pl.ds(pl.multiple_of(i * TILE, TILE), TILE)
-        for j, part in enumerate(thirds(query[:, cols])):
-            query3[j * rank:(j + 1) * rank, cols] = part
-
-    def fold3(v):
-        return v[:rank] + (v[rank:2 * rank] + v[2 * rank:])
-
-    gq_cols = pl.ds(pl.multiple_of(slot * slice_rows, slice_rows), slice_rows)
-    gq[:, gq_cols] = fold3(dot(query3[...], gslice[...], 1, 1))
+        parts = jnp.concatenate(thirds(query[:, cols]), axis=0)
+        query3[:, cols] = parts
+        gq[:, gq_cols] += fold3(dot(parts, gslice[:, cols], 1, 1))
+
     pl.semaphore_wait(barrier, n_greet)
     to_plane("z", "x", lambda dev, _: remote(gq.at[:, gq_cols], gq.at[:, gq_cols], 0, dev))
+
+    loads[2].wait()
+    left[dp] = jnp.zeros((rank, rows), F32)
+
+    @pl.loop(0, n_tiles)
+    def _(i):
+        cols = pl.ds(pl.multiple_of(i * TILE, TILE), TILE)
+        left[dp] += fold3(dot(query3[:, cols], res[:, cols], 1, 1))
+
+    loads[3].wait()
 
     def tile(i):
         cols = pl.ds(pl.multiple_of(i * TILE, TILE), TILE)
         tile_load(i).wait()
-        product = dot(act[...], gbuf[lax.rem(i, 2)], 0, 0)
+        product = dot(act[...], gbuf[lax.rem(i, SLOTS)], 0, 0)
         merged[:, cols] = product + res[:, cols].astype(F32)
 
-        @pl.when(i + 2 < n_tiles)
+        @pl.when(i + SLOTS < n_tiles)
         def _():
-            tile_load(i + 2).start()
+            tile_load(i + SLOTS).start()
 
     def gq_core():
         arrived(lambda: gq.at[:, pl.ds(0, (n_plane - 1) * slice_rows)], 0)
@@ -163,9 +171,13 @@
 
     def left_factor():
         arrived(lambda: gq.at[:, pl.ds(0, n_plane * slice_rows)], 1)
-        total = fold3(dot(query3[...], res[...], 1, 1))
-        total += fold3(dot(jnp.concatenate(thirds(gq[...]), axis=0), act[...], 1, 0))
-        left[dp] = total
+        step = tokens // 4
+
+        @pl.loop(0, 4)
+        def _(i):
+            part = pl.ds(pl.multiple_of(i * step, step), step)
+            left[dp] += fold3(dot(jnp.concatenate(thirds(gq[:, part]), axis=0), act[part, :], 1, 0))
+
         to_line("y", lambda dev, _: remote(left.at[dp], left.at[dp], 2, dev))
 
     def average():
@@ -187,18 +199,19 @@
         gram_slots[chip] = gram_out[...] + gram_in[...]
         to_plane("z", "x", lambda dev, _: remote(gram_slots.at[chip], gram_slots.at[chip], 4, dev))
 
-    def right_terms(g):
+    def right_terms(groups):
         step = 512
 
-        @pl.loop(0, gcols // step)
+        @pl.loop(groups[0] * gcols // step, (groups[-1] + 1) * gcols // step)
         def _(i):
-            cols = pl.ds(pl.multiple_of(gcols * g + i * step, step), step)
+            cols = pl.ds(pl.multiple_of(i * step, step), step)
             high, low = halves(merged[:, cols])
             both = dot(avg2[...], high, 1, 0)
             tt[:, cols] = both[:rank] + (both[rank:] + dot(avg2[:rank], low, 1, 0))
 
         theirs = pl.ds(pl.multiple_of(half * (1 - core), half), half)
-        remote(tt.at[theirs, at_group(g)], core_rx.at[:, at_group(g)], sem_of(g, "core"), partner)
+        for g in groups:
+            remote(tt.at[theirs, at_group(g)], core_rx.at[:, at_group(g)], sem_of(g, "core"), partner)
 
     def line_of(g):
         axis = AXES[g]
@@ -210,11 +223,43 @@
     def part_rows(p, size):
         return pl.ds(pl.multiple_of(p * size, size), size)
 
-    def line_send(g):
-        axis, _, _, n, lrows, *_ = line_of(g)
+    def core_sum(g):
         cols = at_group(g)
         arrived(lambda: core_rx.at[:, cols], sem_of(g, "core"))
         core_rx[:, cols] = core_rx[:, cols] + tt[part_rows(core, half), cols]
+        return cols
+
+    n_col = gcols // 128
+    l_group = GROUPS - 1
+    l_rows = half * gcols // (128 * n_chips)
+
+    def last_piece(at, top):
+        return (pl.ds(pl.multiple_of(top + at // n_col * l_rows, l_rows), l_rows),
+                pl.ds(pl.multiple_of(gcols * l_group + at % n_col * 128, 128), 128))
+
+    def last_send():
+        core_sum(l_group)
+        to_all(lambda dev, p: remote(
+            core_rx.at[last_piece(p, 0)], last_rx.at[:, part_rows(place, 128)], sem_of(l_group, "line"), dev))
+
+    def last_gather():
+        arrived(lambda: last_rx.at[:, pl.ds(0, (n_chips - 1) * 128)], sem_of(l_group, "line"))
+        last_rx[:, part_rows(place, 128)] = core_rx[last_piece(place, 0)]
+        total = last_rx[:, 0:128]
+        for k in range(1, n_chips):
+            total = total + last_rx[:, k * 128:(k + 1) * 128]
+        piece = last_piece(place, half * core)
+        tf[piece] = total
+        to_all(lambda dev, _: remote(tf.at[piece], tf.at[piece], sem_of(l_group, "ag_line"), dev))
+
+    def last_core():
+        arrived(lambda: tf.at[pl.ds(0, l_rows), pl.ds(0, (n_chips - 1) * 128)], sem_of(l_group, "ag_line"))
+        mine = tf.at[part_rows(core, half), at_group(l_group)]
+        remote(mine, mine, sem_of(l_group, "ag_core"), partner)
+
+    def line_send(g):
+        axis, _, _, n, lrows, *_ = line_of(g)
+        cols = core_sum(g)
         to_line(axis, lambda dev, p: remote(
             core_rx.at[part_rows(p, lrows), cols], line_rx.at[g, part_rows(me[axis], lrows)], sem_of(g, "line"), dev))
 
@@ -284,46 +329,29 @@
         wl3[rank:2 * rank] = high
         wl3[2 * rank:] = low
 
-    def out_copies(g):
-        return [pltpu.make_async_copy(res.at[:, at_group(g)], error_hbm.at[:, at_group(g)], store.at[g, 0]),
-                pltpu.make_async_copy(right.at[:, at_group(g)], right_hbm.at[:, at_group(g)], store.at[g, 1])]
-
-    def finish(g):
+    def finish(groups):
         step = 512
-        arrived(lambda: tf.at[pl.ds(0, half), at_group(g)], sem_of(g, "ag_core"))
-
-        @pl.loop(0, gcols // step)
+        for g in groups:
+            arrived(lambda g=g: tf.at[pl.ds(0, half), at_group(g)], sem_of(g, "ag_core"))
+
+        @pl.loop(groups[0] * gcols // step, (groups[-1] + 1) * gcols // step)
         def _(i):
-            cols = pl.ds(pl.multiple_of(gcols * g + i * step, step), step)
+            cols = pl.ds(pl.multiple_of(i * step, step), step)
             high, low = halves(tf[:, cols])
             both = dot(wl3[...], jnp.concatenate([high, low, high], axis=0), 0, 0)
             res[:, cols] = (merged[:, cols] - both[:rows]).astype(BF16)
             right[:, cols] = both[rows:rows + rank]
 
-        for c in out_copies(g):
-            c.start()
-
-    loads[2].wait()
-    loads[3].wait()
-    early = range(GROUPS - 1)
-    last = GROUPS - 1
+    early = list(range(l_group))
 
     def after_5():
         average()
-        for g in early:
-            right_terms(g)
-
-    def after_6():
+        right_terms(early)
         gram_sum()
         for g in early:
             line_send(g)
 
-    def after_7():
-        right_terms(last)
-        for g in early:
-            plane_send(g)
-
-    stages = {2: gq_core, 3: left_factor, 5: after_5, 6: after_6, 7: after_7}
+    stages = {2: gq_core, 3: left_factor, 5: after_5}
 
     @pl.loop(0, n_tiles)
     def _(i):
@@ -331,24 +359,21 @@
         for at, stage in stages.items():
             pl.when(i == at)(stage)
 
-    line_send(last)
+    right_terms([l_group])
+    last_send()
+    for g in early:
+        plane_send(g)
+    cholesky()
     for g in early:
         gather_plane(g)
-    plane_send(last)
+    last_gather()
     for g in early:
         gather_line(g)
-    cholesky()
-    gather_plane(last)
+    last_core()
     for g in early:
         gather_core(g)
-    gather_line(last)
-    for g in early:
-        finish(g)
-    gather_core(last)
-    finish(last)
-    for g in range(GROUPS):
-        for c in out_copies(g):
-            c.wait()
+    finish([l_group])
+    finish(early)
     for view, sem in sent:
         pltpu.make_async_copy(view(), view(), send.at[sem]).wait()
 
@@ -367,14 +392,12 @@
         lmax = half // min(sizes.values())
         error, right_t = pl.pallas_call(
             functools.partial(kernel, sizes),
-            out_shape=(jax.ShapeDtypeStruct((rows, width), BF16), jax.ShapeDtypeStruct((rank, width), F32)),
+            out_shape=(pltpu.VMEM((rows, width), BF16), pltpu.VMEM((rank, width), F32)),
             in_specs=[pl.BlockSpec(memory_space=pl.ANY)] * 4,
-            out_specs=(pl.BlockSpec(memory_space=pl.ANY),) * 2,
+            out_specs=(pl.BlockSpec(memory_space=pltpu.VMEM),) * 2,
             scratch_shapes=[
                 pltpu.VMEM((tokens, rows), BF16),
-                pltpu.VMEM((2, tokens, TILE), BF16),
-                pltpu.VMEM((rows, width), BF16),
-                pltpu.VMEM((rank, width), F32),
+                pltpu.VMEM((SLOTS, tokens, TILE), BF16),
                 pltpu.VMEM((3 * rank, width), BF16),
                 pltpu.VMEM((tokens // (2 * n_plane), width), BF16),
                 pltpu.VMEM((rows, width), F32),
@@ -392,16 +415,15 @@
                 pltpu.VMEM((GROUPS, half, gcols), F32),
                 pltpu.VMEM((GROUPS, lmax, gcols), F32),
                 pltpu.VMEM((GROUPS, lmax, gcols), F32),
-                pltpu.VMEM((rank, width), F32),
+                pltpu.VMEM((half * gcols // (128 * sizes["y"] * n_plane), sizes["y"] * n_plane * 128), F32),
                 pltpu.VMEM((rank, width), F32),
                 pltpu.SemaphoreType.DMA((N_SEMS,)),
                 pltpu.SemaphoreType.DMA((N_SEMS,)),
                 pltpu.SemaphoreType.DMA((4,)),
-                pltpu.SemaphoreType.DMA((2,)),
-                pltpu.SemaphoreType.DMA((GROUPS, 2)),
+                pltpu.SemaphoreType.DMA((SLOTS,)),
             ],
             compiler_params=pltpu.CompilerParams(
-                collective_id=0, has_side_effects=True, vmem_limit_bytes=60 * 2**20
+                collective_id=0, has_side_effects=True, vmem_limit_bytes=52 * 2**20
             ),
             name="powersgd",
         )(activations, out_grads, residual, query_factor.T)

time: 83.1 us -> 74.5 us (0.90)
  Pallas kernels: 76.2 us -> 70.5 us
  local copies, waits for them, and re-layouts: 6.11 us -> 3.33 us
    pallas_call x1, Pallas kernels: 76.2 us -> 70.5 us  [on_device(): pl.pallas_call(functools.partial(kernel, sizes), out_shape=(pltpu.VMEM((r...]
    unnamed x4 -> x2, local copies, waits for them, and re-layouts: 6.11 us -> 3.33 us
where the time goes in v2:
time: 74.5 us; the launch traced here: 74.4 us
  Pallas kernels  70.5 us (95%)
  local copies, waits for them, and re-layouts  3.33 us (4%)
    pallas_call x1, Pallas kernels, on_device(): pl.pallas_call(functools.partial(kernel, sizes), out_shape=(pltpu.VMEM((r...  70.5 us
    unnamed x2, local copies, waits for them, and re-layouts  3.33 us

profile of v2, /device:TPU:1, one launch (start us, length us, event | category | flops | bytes accessed | tf_op | source)
XLA Modules:
  0.0 74.4 jit_solution(2912724245522258877)
XLA Ops:
  0.6 70.5 %powersgd.1 = (bf16[256,8192]{1,0:T(8,128)(2,1)S(1)}, f32[64,8192]{1,0:T(8,128)S(1)}) custom-call(bf16[4096,256]{1,0:T(8,128)(2,1)} %act_hbm.1, bf16[4096,8192]{1,0:T(8,128)(2,1)} %grad_hbm.1, bf16[256,8192]{1,0:T(8,128)(2,1)} %res_hbm.1, f32[64,8192]{1,0:T(8,128)} %bitcast.3), custom_call_target="tpu_custom_call" | custom-call | tf_op jit(solution)/shard_map/powersgd/pallas_call | solution.py:393
  71.1 2.0 %copy.8 = bf16[256,8192]{1,0:T(8,128)(2,1)} copy(bf16[256,8192]{1,0:T(8,128)(2,1)S(1)} %get-tuple-element.6) | data formatting | bytes 8388608
  73.1 1.3 %copy.9 = f32[8192,64]{0,1:T(8,128)} copy(f32[8192,64]{0,1:T(8,128)S(1)} %bitcast.2) | data formatting | bytes 4194304

commit v3 on v2

--- a/solution.py
+++ b/solution.py
@@ -107,13 +107,19 @@
         pltpu.make_async_copy(act_hbm, act, load.at[3]),
     ]
 
+    def first_load(j):
+        cols = pl.ds(pl.multiple_of(j * (TILE // 2), TILE // 2), TILE // 2)
+        return pltpu.make_async_copy(grad_hbm.at[:, cols], gbuf.at[0, :, cols], gload.at[SLOTS + j])
+
     def tile_load(i):
         b = lax.rem(i, SLOTS)
         return pltpu.make_async_copy(grad_hbm.at[:, pl.ds(pl.multiple_of(i * TILE, TILE), TILE)], gbuf.at[b], gload.at[b])
 
     for c in loads:
         c.start()
-    for b in range(SLOTS):
+    for j in range(2):
+        first_load(j).start()
+    for b in range(1, SLOTS):
         tile_load(b).start()
 
     barrier = pltpu.get_barrier_semaphore()
@@ -153,6 +159,14 @@
         left[dp] += fold3(dot(query3[:, cols], res[:, cols], 1, 1))
 
     loads[3].wait()
+
+    @pl.loop(0, 2)
+    def _(j):
+        cols = pl.ds(pl.multiple_of(j * (TILE // 2), TILE // 2), TILE // 2)
+        first_load(j).wait()
+        merged[:, cols] = dot(act[...], gbuf[0, :, cols], 0, 0) + res[:, cols].astype(F32)
+
+    tile_load(SLOTS).start()
 
     def tile(i):
         cols = pl.ds(pl.multiple_of(i * TILE, TILE), TILE)
@@ -329,12 +343,11 @@
         wl3[rank:2 * rank] = high
         wl3[2 * rank:] = low
 
-    def finish(groups):
+    def finish(g):
         step = 512
-        for g in groups:
-            arrived(lambda g=g: tf.at[pl.ds(0, half), at_group(g)], sem_of(g, "ag_core"))
-
-        @pl.loop(groups[0] * gcols // step, (groups[-1] + 1) * gcols // step)
+        arrived(lambda: tf.at[pl.ds(0, half), at_group(g)], sem_of(g, "ag_core"))
+
+        @pl.loop(g * gcols // step, (g + 1) * gcols // step)
         def _(i):
             cols = pl.ds(pl.multiple_of(i * step, step), step)
             high, low = halves(tf[:, cols])
@@ -347,13 +360,15 @@
     def after_5():
         average()
         right_terms(early)
+
+    def after_6():
         gram_sum()
         for g in early:
             line_send(g)
 
-    stages = {2: gq_core, 3: left_factor, 5: after_5}
-
-    @pl.loop(0, n_tiles)
+    stages = {2: gq_core, 3: left_factor, 5: after_5, 6: after_6}
+
+    @pl.loop(1, n_tiles)
     def _(i):
         tile(i)
         for at, stage in stages.items():
@@ -372,8 +387,8 @@
     last_core()
     for g in early:
         gather_core(g)
-    finish([l_group])
-    finish(early)
+    for g in [l_group] + early:
+        finish(g)
     for view, sem in sent:
         pltpu.make_async_copy(view(), view(), send.at[sem]).wait()
 
@@ -420,7 +435,7 @@
                 pltpu.SemaphoreType.DMA((N_SEMS,)),
                 pltpu.SemaphoreType.DMA((N_SEMS,)),
                 pltpu.SemaphoreType.DMA((4,)),
-                pltpu.SemaphoreType.DMA((SLOTS,)),
+                pltpu.SemaphoreType.DMA((SLOTS + 2,)),
             ],
             compiler_params=pltpu.CompilerParams(
                 collective_id=0, has_side_effects=True, vmem_limit_bytes=52 * 2**20

time: 74.5 us -> 75.3 us (1.011)
  no operation moved by 1% of the time
where the time goes in v3:
time: 75.3 us; the launch traced here: 75.1 us
  Pallas kernels  71.2 us (95%)
  local copies, waits for them, and re-layouts  3.33 us (4%)
    pallas_call x1, Pallas kernels, on_device(): pl.pallas_call(functools.partial(kernel, sizes), out_shape=(pltpu.VMEM((r...  71.2 us
    unnamed x2, local copies, waits for them, and re-layouts  3.33 us

profile of v3, /device:TPU:1, one launch (start us, length us, event | category | flops | bytes accessed | tf_op | source)
XLA Modules:
  0.0 75.1 jit_solution(16166591103228408058)
XLA Ops:
  0.6 71.2 %powersgd.1 = (bf16[256,8192]{1,0:T(8,128)(2,1)S(1)}, f32[64,8192]{1,0:T(8,128)S(1)}) custom-call(bf16[4096,256]{1,0:T(8,128)(2,1)} %act_hbm.1, bf16[4096,8192]{1,0:T(8,128)(2,1)} %grad_hbm.1, bf16[256,8192]{1,0:T(8,128)(2,1)} %res_hbm.1, f32[64,8192]{1,0:T(8,128)} %bitcast.3), custom_call_target="tpu_custom_call" | custom-call | tf_op jit(solution)/shard_map/powersgd/pallas_call | solution.py:408
  71.8 2.0 %copy.8 = bf16[256,8192]{1,0:T(8,128)(2,1)} copy(bf16[256,8192]{1,0:T(8,128)(2,1)S(1)} %get-tuple-element.6) | data formatting | bytes 8388608
  73.8 1.3 %copy.9 = f32[8192,64]{0,1:T(8,128)} copy(f32[8192,64]{0,1:T(8,128)S(1)} %bitcast.2) | data formatting | bytes 4194304

commit v4 on v3

--- a/solution.py
+++ b/solution.py
@@ -76,10 +76,16 @@
             act_on(device(**{axis: p}), p)
 
     def to_all(act_on):
-        @pl.loop(1, n_chips)
-        def _(k):
-            y, z, x = shift("y", k // n_plane), shift("z", (k // nx) % nz), shift("x", k % nx)
+        home = ((ny - ny // 2) * nz + nz - nz // 2) * nx + nx - nx // 2
+
+        def step(k):
+            y = shift("y", k // n_plane + ny // 2)
+            z = shift("z", (k // nx) % nz + nz // 2)
+            x = shift("x", k % nx + nx // 2)
             act_on(device(y=y, z=z, x=x), (y * nz + z) * nx + x)
+
+        pl.loop(0, home)(step)
+        pl.loop(home + 1, n_chips)(step)
 
     sent = []
 
@@ -151,13 +157,6 @@
     to_plane("z", "x", lambda dev, _: remote(gq.at[:, gq_cols], gq.at[:, gq_cols], 0, dev))
 
     loads[2].wait()
-    left[dp] = jnp.zeros((rank, rows), F32)
-
-    @pl.loop(0, n_tiles)
-    def _(i):
-        cols = pl.ds(pl.multiple_of(i * TILE, TILE), TILE)
-        left[dp] += fold3(dot(query3[:, cols], res[:, cols], 1, 1))
-
     loads[3].wait()
 
     @pl.loop(0, 2)
@@ -184,6 +183,13 @@
         remote(mine, mine, 1, partner)
 
     def left_factor():
+        left[dp] = jnp.zeros((rank, rows), F32)
+
+        @pl.loop(0, n_tiles)
+        def _(i):
+            cols = pl.ds(pl.multiple_of(i * TILE, TILE), TILE)
+            left[dp] += fold3(dot(query3[:, cols], res[:, cols], 1, 1))
+
         arrived(lambda: gq.at[:, pl.ds(0, n_plane * slice_rows)], 1)
         step = tokens // 4
 
@@ -214,7 +220,7 @@
         to_plane("z", "x", lambda dev, _: remote(gram_slots.at[chip], gram_slots.at[chip], 4, dev))
 
     def right_terms(groups):
-        step = 512
+        step = 2048
 
         @pl.loop(groups[0] * gcols // step, (groups[-1] + 1) * gcols // step)
         def _(i):
@@ -314,28 +320,30 @@
         mine = tf.at[part_rows(core, half), at_group(g)]
         remote(mine, mine, sem_of(g, "ag_core"), partner)
 
-    def cholesky():
+    at_row = lax.broadcasted_iota(jnp.int32, (rank, 1), 0)
+    at_lane = lax.broadcasted_iota(jnp.int32, (1, 2 * rank), 1)
+
+    def factor_start():
         arrived(lambda: gram_slots.at[pl.ds(0, n_plane - 1)], 4)
         packed = gram_slots[0]
         for k in range(1, n_plane):
             packed = packed + gram_slots[k]
         gram = jnp.concatenate([packed[:, :rank], packed[:, rank:]], axis=0)
-        at_row = lax.broadcasted_iota(jnp.int32, (rank, 1), 0)
-        at_lane = lax.broadcasted_iota(jnp.int32, (1, 2 * rank), 1)
         unit = (lax.broadcasted_iota(jnp.int32, (rank, rank), 0) == lax.broadcasted_iota(jnp.int32, (rank, rank), 1)).astype(F32)
         chol[...] = jnp.concatenate([gram, unit], axis=1)
 
-        @pl.loop(0, rank)
+    def factor(start, stop):
+        @pl.loop(start, stop)
         def _(k):
             matrix = chol[...]
             row = chol[pl.ds(k, 1), :]
             column = jnp.sum(jnp.where(at_lane == k, matrix, 0.0), axis=1, keepdims=True)
             pivot = jnp.sum(jnp.where(at_lane == k, row, 0.0), axis=1, keepdims=True)
-            scale = 1.0 / jnp.sqrt(pivot)
-            row = row * scale
-            chol[...] = jnp.where(at_row == k, row, matrix - jnp.where(at_row > k, column * scale, 0.0) * row)
-
-        inverse = chol[:, rank:]
+            chol[...] = matrix - jnp.where(at_row > k, column, 0.0) * (row * (1.0 / pivot))
+
+    def factor_end():
+        pivots = jnp.sum(jnp.where(at_row == at_lane, chol[...], 0.0), axis=1, keepdims=True)
+        inverse = chol[:, rank:] * (1.0 / jnp.sqrt(pivots))
         orth = dot(inverse, avg[...], 1, 0, HIGHEST)
         both = jnp.concatenate([dot(inverse, orth, 0, 0, HIGHEST), inverse.T, jnp.zeros((rank, rank), F32)], axis=1)
         high, low = halves(both * (1.0 / ny))
@@ -344,7 +352,7 @@
         wl3[2 * rank:] = low
 
     def finish(g):
-        step = 512
+        step = 1024
         arrived(lambda: tf.at[pl.ds(0, half), at_group(g)], sem_of(g, "ag_core"))
 
         @pl.loop(g * gcols // step, (g + 1) * gcols // step)
@@ -359,14 +367,17 @@
 
     def after_5():
         average()
-        right_terms(early)
-
-    def after_6():
+        for g in early:
+            right_terms([g])
         gram_sum()
         for g in early:
             line_send(g)
 
-    stages = {2: gq_core, 3: left_factor, 5: after_5, 6: after_6}
+    def after_2():
+        gq_core()
+        left_factor()
+
+    stages = {2: after_2, 5: after_5}
 
     @pl.loop(1, n_tiles)
     def _(i):
@@ -375,22 +386,40 @@
             pl.when(i == at)(stage)
 
     right_terms([l_group])
+    plane_send(0)
+    plane_send(1)
+    plane_send(2)
     last_send()
-    for g in early:
-        plane_send(g)
-    cholesky()
-    for g in early:
-        gather_plane(g)
+    factor_start()
+    factor(0, rank // 4)
+    gather_plane(0)
+    gather_plane(1)
+    gather_plane(2)
     last_gather()
-    for g in early:
-        gather_line(g)
+    factor(rank // 4, rank // 2)
+    gather_line(0)
+    gather_line(1)
+    gather_line(2)
+    factor(rank // 2, rank)
+    factor_end()
+    gather_core(0)
+    gather_core(1)
+    gather_core(2)
     last_core()
-    for g in early:
-        gather_core(g)
-    for g in [l_group] + early:
-        finish(g)
+    finish(0)
+    finish(1)
+    finish(2)
+    finish(l_group)
     for view, sem in sent:
         pltpu.make_async_copy(view(), view(), send.at[sem]).wait()
+
+
+def write_kernel(error, right, error_hbm, right_hbm, sem):
+    copies = [pltpu.make_async_copy(error, error_hbm, sem.at[0]), pltpu.make_async_copy(right, right_hbm, sem.at[1])]
+    for c in copies:
+        c.start()
+    for c in copies:
+        c.wait()
 
 
 def solution(mesh):
@@ -442,6 +471,15 @@
             ),
             name="powersgd",
         )(activations, out_grads, residual, query_factor.T)
+        error, right_t = pl.pallas_call(
+            write_kernel,
+            out_shape=(jax.ShapeDtypeStruct((rows, width), BF16), jax.ShapeDtypeStruct((rank, width), F32)),
+            in_specs=[pl.BlockSpec(memory_space=pltpu.VMEM)] * 2,
+            out_specs=(pl.BlockSpec(memory_space=pl.ANY),) * 2,
+            scratch_shapes=[pltpu.SemaphoreType.DMA((2,))],
+            compiler_params=pltpu.CompilerParams(vmem_limit_bytes=16 * 2**20),
+            name="write_out",
+        )(pltpu.with_memory_space_constraint(error, pltpu.VMEM), pltpu.with_memory_space_constraint(right_t, pltpu.VMEM))
         return error, right_t.T
 
     return jax.shard_map(

time: 75.3 us -> 71 us (0.943)
  local copies, waits for them, and re-layouts: 3.33 us -> 0 us
  Pallas kernels: 71.2 us -> 70.3 us
    pallas_call x1, Pallas kernels: 71.2 us -> 67.6 us  [on_device(): pl.pallas_call(functools.partial(kernel, sizes), out_shape=(pltpu.VMEM((r...]
    unnamed x2 -> x0, local copies, waits for them, and re-layouts: 3.33 us -> none
    pallas_call x0 -> x1, Pallas kernels: none -> 2.72 us  [on_device(): pl.pallas_call(write_kernel, out_shape=(jax.ShapeDtypeStruct((rows, width...]
where the time goes in v4:
time: 71 us; the launch traced here: 70.9 us
  Pallas kernels  70.3 us (99%)
    pallas_call x1, Pallas kernels, on_device(): pl.pallas_call(functools.partial(kernel, sizes), out_shape=(pltpu.VMEM((r...  67.6 us
    pallas_call x1, Pallas kernels, on_device(): pl.pallas_call(write_kernel, out_shape=(jax.ShapeDtypeStruct((rows, width...  2.72 us

profile of v4, /device:TPU:1, one launch (start us, length us, event | category | flops | bytes accessed | tf_op | source)
XLA Modules:
  0.0 70.9 jit_solution(9663866966863854443)
XLA Ops:
  0.6 67.6 %powersgd.1 = (bf16[256,8192]{1,0:T(8,128)(2,1)S(1)}, f32[64,8192]{1,0:T(8,128)S(1)}) custom-call(bf16[4096,256]{1,0:T(8,128)(2,1)} %act_hbm.1, bf16[4096,8192]{1,0:T(8,128)(2,1)} %grad_hbm.1, bf16[256,8192]{1,0:T(8,128)(2,1)} %res_hbm.1, f32[64,8192]{1,0:T(8,128)} %bitcast.2), custom_call_target="tpu_custom_call" | custom-call | tf_op jit(solution)/shard_map/powersgd/pallas_call | solution.py:437
  68.2 2.7 %write_out.1 = (bf16[256,8192]{1,0:T(8,128)(2,1)}, f32[64,8192]{1,0:T(8,128)}) custom-call(bf16[256,8192]{1,0:T(8,128)(2,1)S(1)} %get-tuple-element.6.error, f32[64,8192]{1,0:T(8,128)S(1)} %get-tuple-element.7.right), custom_call_target="tpu_custom_call" | custom-call | tf_op jit(solution)/shard_map/write_out/pallas_call | solution.py:474

commit v5 on v4

--- a/solution.py
+++ b/solution.py
@@ -34,10 +34,9 @@
     return lax.dot_general(a, b, (((ca,), (cb,)), ((), ())), precision=precision, preferred_element_type=F32)
 
 
-def kernel(sizes, act_hbm, grad_hbm, res_hbm, query_hbm, res, right,
-           act, gbuf, query3, gslice, merged, gq, left, avg, avg2, gram_in, gram_out, gram_slots, chol,
-           wl3, tt, core_rx, line_rx, line_sum, plane_rx, last_rx, tf, send, recv, load, gload):
-    query = right
+def kernel(sizes, act_hbm, grad_hbm, res_hbm, query_hbm, merged, terms3, wl3,
+           act, gbuf, res, query, query3, gslice, gq, left, avg, avg2, gram_in, gram_out, gram_slots, chol,
+           tt, core_rx, line_rx, line_sum, plane_rx, last_rx, tf, send, recv, load, gload):
     ny, nz, nx = sizes["y"], sizes["z"], sizes["x"]
     dp, tp = lax.axis_index("dp"), lax.axis_index("tp")
     me = {"y": dp, "z": tp // (2 * nx), "x": (tp // 2) % nx}
@@ -47,6 +46,7 @@
     n_tiles = width // TILE
     gcols = width // GROUPS
     half = rank // 2
+    wide = 2048
 
     def device(**to):
         at = {**me, "c": core, **to}
@@ -146,9 +146,9 @@
     gq_cols = pl.ds(pl.multiple_of(slot * slice_rows, slice_rows), slice_rows)
     gq[:, gq_cols] = jnp.zeros((rank, slice_rows), F32)
 
-    @pl.loop(0, n_tiles)
+    @pl.loop(0, width // wide)
     def _(i):
-        cols = pl.ds(pl.multiple_of(i * TILE, TILE), TILE)
+        cols = pl.ds(pl.multiple_of(i * wide, wide), wide)
         parts = jnp.concatenate(thirds(query[:, cols]), axis=0)
         query3[:, cols] = parts
         gq[:, gq_cols] += fold3(dot(parts, gslice[:, cols], 1, 1))
@@ -185,15 +185,15 @@
     def left_factor():
         left[dp] = jnp.zeros((rank, rows), F32)
 
-        @pl.loop(0, n_tiles)
+        @pl.loop(0, width // wide)
         def _(i):
-            cols = pl.ds(pl.multiple_of(i * TILE, TILE), TILE)
+            cols = pl.ds(pl.multiple_of(i * wide, wide), wide)
             left[dp] += fold3(dot(query3[:, cols], res[:, cols], 1, 1))
 
         arrived(lambda: gq.at[:, pl.ds(0, n_plane * slice_rows)], 1)
-        step = tokens // 4
-
-        @pl.loop(0, 4)
+        step = tokens // 2
+
+        @pl.loop(0, 2)
         def _(i):
             part = pl.ds(pl.multiple_of(i * step, step), step)
             left[dp] += fold3(dot(jnp.concatenate(thirds(gq[:, part]), axis=0), act[part, :], 1, 0))
@@ -352,16 +352,11 @@
         wl3[2 * rank:] = low
 
     def finish(g):
-        step = 1024
         arrived(lambda: tf.at[pl.ds(0, half), at_group(g)], sem_of(g, "ag_core"))
-
-        @pl.loop(g * gcols // step, (g + 1) * gcols // step)
-        def _(i):
-            cols = pl.ds(pl.multiple_of(i * step, step), step)
-            high, low = halves(tf[:, cols])
-            both = dot(wl3[...], jnp.concatenate([high, low, high], axis=0), 0, 0)
-            res[:, cols] = (merged[:, cols] - both[:rows]).astype(BF16)
-            right[:, cols] = both[rows:rows + rank]
+        high, low = halves(tf[:, at_group(g)])
+        terms3[:rank, at_group(g)] = high
+        terms3[rank:2 * rank, at_group(g)] = low
+        terms3[2 * rank:, at_group(g)] = high
 
     early = list(range(l_group))
 
@@ -414,12 +409,26 @@
         pltpu.make_async_copy(view(), view(), send.at[sem]).wait()
 
 
-def write_kernel(error, right, error_hbm, right_hbm, sem):
-    copies = [pltpu.make_async_copy(error, error_hbm, sem.at[0]), pltpu.make_async_copy(right, right_hbm, sem.at[1])]
-    for c in copies:
-        c.start()
-    for c in copies:
-        c.wait()
+def write_kernel(merged, terms3, wl3, error_hbm, right_hbm, error, right, sem):
+    rows, width = merged.shape
+    rank = right.shape[0]
+
+    def copies(i):
+        cols = pl.ds(i * TILE, TILE)
+        return (pltpu.make_async_copy(error.at[:, cols], error_hbm.at[:, cols], sem.at[0, i]),
+                pltpu.make_async_copy(right.at[:, cols], right_hbm.at[:, cols], sem.at[1, i]))
+
+    for i in range(width // TILE):
+        cols = pl.ds(i * TILE, TILE)
+        both = dot(wl3[:, :rows + rank], terms3[:, cols], 0, 0)
+        error[:, cols] = (merged[:, cols] - both[:rows]).astype(BF16)
+        right[:, cols] = both[rows:rows + rank]
+        for c in copies(i):
+            c.start()
+
+    for i in range(width // TILE):
+        for c in copies(i):
+            c.wait()
 
 
 def solution(mesh):
@@ -434,17 +443,22 @@
         gcols = width // GROUPS
         n_plane = sizes["z"] * sizes["x"]
         lmax = half // min(sizes.values())
-        error, right_t = pl.pallas_call(
+        merged, terms3, wl3 = pl.pallas_call(
             functools.partial(kernel, sizes),
-            out_shape=(pltpu.VMEM((rows, width), BF16), pltpu.VMEM((rank, width), F32)),
+            out_shape=(
+                pltpu.VMEM((rows, width), F32),
+                pltpu.VMEM((3 * rank, width), BF16),
+                pltpu.VMEM((3 * rank, rows + 2 * rank), BF16),
+            ),
             in_specs=[pl.BlockSpec(memory_space=pl.ANY)] * 4,
-            out_specs=(pl.BlockSpec(memory_space=pltpu.VMEM),) * 2,
+            out_specs=(pl.BlockSpec(memory_space=pltpu.VMEM),) * 3,
             scratch_shapes=[
                 pltpu.VMEM((tokens, rows), BF16),
                 pltpu.VMEM((SLOTS, tokens, TILE), BF16),
+                pltpu.VMEM((rows, width), BF16),
+                pltpu.VMEM((rank, width), F32),
                 pltpu.VMEM((3 * rank, width), BF16),
                 pltpu.VMEM((tokens // (2 * n_plane), width), BF16),
-                pltpu.VMEM((rows, width), F32),
                 pltpu.VMEM((rank, tokens), F32),
                 pltpu.VMEM((n_dp, rank, rows), F32),
                 pltpu.VMEM((rank, rows), F32),
@@ -453,7 +467,6 @@
                 pltpu.VMEM((half, 2 * rank), F32),
                 pltpu.VMEM((n_plane, half, 2 * rank), F32),
                 pltpu.VMEM((rank, 2 * rank), F32),
-                pltpu.VMEM((3 * rank, rows + 2 * rank), BF16),
                 pltpu.VMEM((rank, width), F32),
                 pltpu.VMEM((half, width), F32),
                 pltpu.VMEM((GROUPS, half, gcols), F32),
@@ -467,19 +480,23 @@
                 pltpu.SemaphoreType.DMA((SLOTS + 2,)),
             ],
             compiler_params=pltpu.CompilerParams(
-                collective_id=0, has_side_effects=True, vmem_limit_bytes=52 * 2**20
+                collective_id=0, has_side_effects=True, vmem_limit_bytes=50 * 2**20
             ),
             name="powersgd",
         )(activations, out_grads, residual, query_factor.T)
         error, right_t = pl.pallas_call(
             write_kernel,
             out_shape=(jax.ShapeDtypeStruct((rows, width), BF16), jax.ShapeDtypeStruct((rank, width), F32)),
-            in_specs=[pl.BlockSpec(memory_space=pltpu.VMEM)] * 2,
+            in_specs=[pl.BlockSpec(memory_space=pltpu.VMEM)] * 3,
             out_specs=(pl.BlockSpec(memory_space=pl.ANY),) * 2,
-            scratch_shapes=[pltpu.SemaphoreType.DMA((2,))],
-            compiler_params=pltpu.CompilerParams(vmem_limit_bytes=16 * 2**20),
-            name="write_out",
-        )(pltpu.with_memory_space_constraint(error, pltpu.VMEM), pltpu.with_memory_space_constraint(right_t, pltpu.VMEM))
+            scratch_shapes=[
+                pltpu.VMEM((rows, width), BF16),
+                pltpu.VMEM((rank, width), F32),
+                pltpu.SemaphoreType.DMA((2, width // TILE)),
+            ],
+            compiler_params=pltpu.CompilerParams(vmem_limit_bytes=24 * 2**20),
+            name="finish",
+        )(*(pltpu.with_memory_space_constraint(v, pltpu.VMEM) for v in (merged, terms3, wl3)))
         return error, right_t.T
 
     return jax.shard_map(

time: 71 us -> 68.3 us (0.962)
  Pallas kernels: 70.3 us -> 67.5 us
    pallas_call x1, Pallas kernels: 67.6 us -> 64.4 us  [on_device(): pl.pallas_call(functools.partial(kernel, sizes), out_shape=(pltpu.VMEM((r...]
where the time goes in v5:
time: 68.3 us; the launch traced here: 68.2 us
  Pallas kernels  67.5 us (99%)
    pallas_call x1, Pallas kernels, on_device(): pl.pallas_call(functools.partial(kernel, sizes), out_shape=(pltpu.VMEM((r...  64.4 us
    pallas_call x1, Pallas kernels, on_device(): pl.pallas_call(write_kernel, out_shape=(jax.ShapeDtypeStruct((rows, width...  3.12 us

profile of v5, /device:TPU:1, one launch (start us, length us, event | category | flops | bytes accessed | tf_op | source)
XLA Modules:
  0.0 68.2 jit_solution(708637642895895597)
XLA Ops:
  0.6 64.4 %powersgd.1 = (f32[256,8192]{1,0:T(8,128)S(1)}, bf16[192,8192]{1,0:T(8,128)(2,1)S(1)}, bf16[192,384]{1,0:T(8,128)(2,1)S(1)}) custom-call(bf16[4096,256]{1,0:T(8,128)(2,1)} %act_hbm.1, bf16[4096,8192]{1,0:T(8,128)(2,1)} %grad_hbm.1, bf16[256,8192]{1,0:T(8,128)(2,1)} %res_hbm.1, f32[64,8192]{1,0:T(8,128)} %bitcast.2), custom_call_target="tpu_custom_call" | custom-call | tf_op jit(solution)/shard_map/powersgd/pallas_call | solution.py:446
  65.0 3.1 %finish.1 = (bf16[256,8192]{1,0:T(8,128)(2,1)}, f32[64,8192]{1,0:T(8,128)}) custom-call(f32[256,8192]{1,0:T(8,128)S(1)} %get-tuple-element.7.merged, bf16[192,8192]{1,0:T(8,128)(2,1)S(1)} %get-tuple-element.8.terms3, bf16[192,384]{1,0:T(8,128)(2,1)S(1)} %get-tuple-element.9.wl3), custom_call_target="tpu_custom_call" | custom-call | tf_op jit(solution)/shard_map/finish/pallas_call | solution.py:487

commit v6 on v5

--- a/solution.py
+++ b/solution.py
@@ -62,12 +62,15 @@
     place = dp * n_plane + chip
 
     def to_plane(b1, b2, act_on):
-        n2 = sizes[b2]
-
-        @pl.loop(1, sizes[b1] * n2)
-        def _(k):
-            p1, p2 = shift(b1, k // n2), shift(b2, k % n2)
+        n1, n2 = sizes[b1], sizes[b2]
+        home = (n1 - n1 // 2) * n2 + n2 - n2 // 2
+
+        def step(k):
+            p1, p2 = shift(b1, k // n2 + n1 // 2), shift(b2, k % n2 + n2 // 2)
             act_on(device(**{b1: p1, b2: p2}), p1 * n2 + p2)
+
+        pl.loop(0, home)(step)
+        pl.loop(home + 1, n1 * n2)(step)
 
     def to_line(axis, act_on):
         @pl.loop(1, sizes[axis])
@@ -362,11 +365,13 @@
 
     def after_5():
         average()
-        for g in early:
-            right_terms([g])
+        right_terms([0])
+        right_terms([1])
+        line_send(0)
+        right_terms([2])
+        line_send(1)
         gram_sum()
-        for g in early:
-            line_send(g)
+        line_send(2)
 
     def after_2():
         gq_core()

time: 68.3 us -> 68.5 us (level)
  no operation moved by 1% of the time
where the time goes in v6:
time: 68.5 us; the launch traced here: 68.4 us
  Pallas kernels  67.8 us (99%)
    pallas_call x1, Pallas kernels, on_device(): pl.pallas_call(functools.partial(kernel, sizes), out_shape=(pltpu.VMEM((r...  64.7 us
    pallas_call x1, Pallas kernels, on_device(): pl.pallas_call(write_kernel, out_shape=(jax.ShapeDtypeStruct((rows, width...  3.12 us

profile of v6, /device:TPU:1, one launch (start us, length us, event | category | flops | bytes accessed | tf_op | source)
XLA Modules:
  0.0 68.4 jit_solution(10554202960661397534)
XLA Ops:
  0.6 64.7 %powersgd.1 = (f32[256,8192]{1,0:T(8,128)S(1)}, bf16[192,8192]{1,0:T(8,128)(2,1)S(1)}, bf16[192,384]{1,0:T(8,128)(2,1)S(1)}) custom-call(bf16[4096,256]{1,0:T(8,128)(2,1)} %act_hbm.1, bf16[4096,8192]{1,0:T(8,128)(2,1)} %grad_hbm.1, bf16[256,8192]{1,0:T(8,128)(2,1)} %res_hbm.1, f32[64,8192]{1,0:T(8,128)} %bitcast.2), custom_call_target="tpu_custom_call" | custom-call | tf_op jit(solution)/shard_map/powersgd/pallas_call | solution.py:451
  65.3 3.1 %finish.1 = (bf16[256,8192]{1,0:T(8,128)(2,1)}, f32[64,8192]{1,0:T(8,128)}) custom-call(f32[256,8192]{1,0:T(8,128)S(1)} %get-tuple-element.7.merged, bf16[192,8192]{1,0:T(8,128)(2,1)S(1)} %get-tuple-element.8.terms3, bf16[192,384]{1,0:T(8,128)(2,1)S(1)} %get-tuple-element.9.wl3), custom_call_target="tpu_custom_call" | custom-call | tf_op jit(solution)/shard_map/finish/pallas_call | solution.py:492

commit v7 on v6

--- a/solution.py
+++ b/solution.py
@@ -316,12 +316,18 @@
         arrived(lambda: tf.at[pl.ds(0, lrows), pl.ds(0, (n_p - 1) * pcols)], sem_of(g, "ag_plane"))
         piece = (pl.ds(pl.multiple_of(half * core + lrows * me[axis], lrows), lrows), at_group(g))
         to_line(axis, lambda dev, _: remote(tf.at[piece], tf.at[piece], sem_of(g, "ag_line"), dev))
+        remote(tf.at[piece], tf.at[piece], sem_of(g, "ag_core"), partner)
 
     def gather_core(g):
         axis, b1, b2, n, lrows, *_ = line_of(g)
         arrived(lambda: tf.at[pl.ds(0, (n - 1) * lrows), at_group(g)], sem_of(g, "ag_line"))
-        mine = tf.at[part_rows(core, half), at_group(g)]
-        remote(mine, mine, sem_of(g, "ag_core"), partner)
+
+
+        def forward(_, p):
+            piece = (pl.ds(pl.multiple_of(half * core + lrows * p, lrows), lrows), at_group(g))
+            remote(tf.at[piece], tf.at[piece], sem_of(g, "ag_core"), partner)
+
+        to_line(axis, forward)
 
     at_row = lax.broadcasted_iota(jnp.int32, (rank, 1), 0)
     at_lane = lax.broadcasted_iota(jnp.int32, (1, 2 * rank), 1)

time: 68.5 us -> 68.3 us (level)
  no operation moved by 1% of the time
where the time goes in v7:
time: 68.3 us; the launch traced here: 68.2 us
  Pallas kernels  67.5 us (99%)
    pallas_call x1, Pallas kernels, on_device(): pl.pallas_call(functools.partial(kernel, sizes), out_shape=(pltpu.VMEM((r...  64.4 us
    pallas_call x1, Pallas kernels, on_device(): pl.pallas_call(write_kernel, out_shape=(jax.ShapeDtypeStruct((rows, width...  3.12 us

profile of v7, /device:TPU:1, one launch (start us, length us, event | category | flops | bytes accessed | tf_op | source)
XLA Modules:
  0.0 68.2 jit_solution(2920941169819320447)
XLA Ops:
  0.6 64.4 %powersgd.1 = (f32[256,8192]{1,0:T(8,128)S(1)}, bf16[192,8192]{1,0:T(8,128)(2,1)S(1)}, bf16[192,384]{1,0:T(8,128)(2,1)S(1)}) custom-call(bf16[4096,256]{1,0:T(8,128)(2,1)} %act_hbm.1, bf16[4096,8192]{1,0:T(8,128)(2,1)} %grad_hbm.1, bf16[256,8192]{1,0:T(8,128)(2,1)} %res_hbm.1, f32[64,8192]{1,0:T(8,128)} %bitcast.2), custom_call_target="tpu_custom_call" | custom-call | tf_op jit(solution)/shard_map/powersgd/pallas_call | solution.py:457
  65.0 3.1 %finish.1 = (bf16[256,8192]{1,0:T(8,128)(2,1)}, f32[64,8192]{1,0:T(8,128)}) custom-call(f32[256,8192]{1,0:T(8,128)S(1)} %get-tuple-element.7.merged, bf16[192,8192]{1,0:T(8,128)(2,1)S(1)} %get-tuple-element.8.terms3, bf16[192,384]{1,0:T(8,128)(2,1)S(1)} %get-tuple-element.9.wl3), custom_call_target="tpu_custom_call" | custom-call | tf_op jit(solution)/shard_map/finish/pallas_call | solution.py:498
